TPU v7x, 512 devices: a whole 4x4x16 slice. The times are simulated.
512 devices in a mesh: row: 16 (over x, y), col: 32 (over z, core).
Axes of the slice: x: 4, y: 4, z: 16, core: 2. Of those that a mesh axis runs over, the one named last changes fastest.
Arguments:
- features: bfloat16 [65536, 256], P(('col', 'row')), may hold values from -6 to 6
- weight: bfloat16 [256, 256], replicated, may hold values from -0.375 to 0.375
- tile_values: bfloat16 [16, 32, 32, 128, 128], P('row', 'col'), may hold values from -0.125 to 0.125
- tile_rows: int32 [16, 32, 32], P('row', 'col'), may hold values from 0 to 31, as said below
- tile_cols: int32 [16, 32, 32], P('row', 'col'), may hold values from 0 to 15, as said below
- tile_count: int32 [16, 32], P('row', 'col'), may hold values from 4 to 32, as said below
- cotangent: bfloat16 [65536, 256], P(('row', 'col')), may hold values from -6 to 6
Outputs:
- output: bfloat16 [65536, 256], P(('row', 'col'))
- feature_grad: bfloat16 [65536, 256], P(('col', 'row'))
- weight_grad: float32 [256, 256], replicated
Inputs may be any that keep to these rules, and one draw needn't show every extreme that they name: `tile_rows`: slots of one device name distinct tiles; slots at or beyond tile_count are unused. `tile_cols`: slots of one device name distinct tiles; slots at or beyond tile_count are unused. `tile_count`: some device uses all 32 slots.
All inputs are finite; a program needn't handle non-finite values.
Results may differ from a plain program's by a relative error of at most 0.025.
Values may be sent and summed in bfloat16 or wider, within the bound.
A program may use at most 64 MiB of HBM per device.

v0:
```python
import math

import jax
import jax.numpy as jnp
from jax import lax
from jax.sharding import PartitionSpec as P


def block_terms(
    total, first, block_len, tile_vals, source_idx, target_idx, tile_total, panel_tiles, transposed
):
    values = lax.dynamic_slice_in_dim(tile_vals, first, block_len, 0)
    source = lax.dynamic_slice_in_dim(source_idx, first, block_len, 0)
    target = lax.dynamic_slice_in_dim(target_idx, first, block_len, 0)
    picked = jnp.take(panel_tiles, source, axis=0)
    form = "kji,kjf->kif" if transposed else "kij,kjf->kif"
    products = jnp.einsum(form, values, picked, preferred_element_type=jnp.float32)
    active = (first + jnp.arange(block_len, dtype=jnp.int32) < tile_total).astype(jnp.float32)
    return total.at[target].add(products * active[:, None, None])


def sparse_apply(tile_vals, source_idx, target_idx, tile_total, panel_tiles, out_tiles, transposed):
    slot_total = tile_vals.shape[0]
    block_len = math.gcd(slot_total, 16)
    tile_len = tile_vals.shape[1]
    width = panel_tiles.shape[2]
    initial = jnp.zeros((out_tiles, tile_len, width), jnp.float32)

    def advance(index, total):
        return block_terms(
            total,
            index * block_len,
            block_len,
            tile_vals,
            source_idx,
            target_idx,
            tile_total,
            panel_tiles,
            transposed,
        )

    total = lax.fori_loop(0, slot_total // block_len, advance, initial)
    return total.reshape(out_tiles * tile_len, width)


def on_device(features, weight, tile_values, tile_rows, tile_cols, tile_count, cotangent):
    tile_vals = tile_values.reshape(tile_values.shape[2:])
    row_index = tile_rows.reshape(-1)
    col_index = tile_cols.reshape(-1)
    tile_total = tile_count.reshape(())
    tile_len = tile_vals.shape[1]
    node_rows = features.shape[0]
    width = features.shape[1]
    panel = lax.all_gather(features, "row", axis=0, tiled=True)
    panel_tiles = panel.reshape(-1, tile_len, width)
    row_tiles = node_rows * lax.axis_size("col") // tile_len
    partial_value = sparse_apply(
        tile_vals, col_index, row_index, tile_total, panel_tiles, row_tiles, False
    )
    aggregated = lax.psum_scatter(
        partial_value.astype(jnp.bfloat16), "col", scatter_dimension=0, tiled=True
    )
    preact = jnp.dot(aggregated, weight, preferred_element_type=jnp.float32)
    logistic = jax.nn.sigmoid(preact)
    output = (preact * logistic).astype(jnp.bfloat16)
    pre_grad = (
        cotangent.astype(jnp.float32) * logistic * (1.0 + preact * (1.0 - logistic))
    ).astype(jnp.bfloat16)
    scaling = 1.0 / math.sqrt(node_rows * lax.axis_size("row") * lax.axis_size("col"))
    local_grad = jnp.dot(aggregated.T, pre_grad, preferred_element_type=jnp.float32)
    weight_grad = lax.psum(local_grad, ("row", "col")) * scaling
    aggregate_grad = jnp.dot(pre_grad, weight.T, preferred_element_type=jnp.float32).astype(
        jnp.bfloat16
    )
    grad_block = lax.all_gather(aggregate_grad, "col", axis=0, tiled=True)
    grad_tiles = grad_block.reshape(-1, tile_len, width)
    col_tiles = node_rows * lax.axis_size("row") // tile_len
    back_terms = sparse_apply(
        tile_vals, row_index, col_index, tile_total, grad_tiles, col_tiles, True
    )
    feature_grad = lax.psum_scatter(
        back_terms.astype(jnp.bfloat16), "row", scatter_dimension=0, tiled=True
    )
    return (output, feature_grad, weight_grad)


def solution(mesh):
    return jax.shard_map(
        on_device,
        mesh=mesh,
        in_specs=(
            P(("col", "row"), None),
            P(),
            P("row", "col", None, None, None),
            P("row", "col", None),
            P("row", "col", None),
            P("row", "col"),
            P(("row", "col"), None),
        ),
        out_specs=(P(("row", "col"), None), P(("col", "row"), None), P()),
        check_vma=False,
    )
```

profile of v0, /device:TPU:1, one launch (start us, length us, event | category | flops | bytes accessed | tf_op | source)
XLA Modules:
  0.0 834.5 jit_solution(16814637419433659609)
XLA Ops:
  7.2 0.0 copy-start
  7.2 0.0 all-gather.3.cloned.1.call-start
  7.2 0.7 all-gather.3.cloned.1.call-update
  7.9 0.0 reduce-scatter.3.cloned.1.call-start
  8.0 65.0 %all-gather.3.cloned.1.call-done = bf16[2048,256]{1,0:T(8,128)(2,1)} async-done(((bf16[128,256]{1,0:T(8,128)(2,1)}), bf16[2048,256]{1,0:T(8,128)(2,1)}) %all-gather.3.cloned.1.call-update) | async-done | bytes 1048592 | tf_op jit(solution)/shard_map/all_gather | solution.py:54
  73.0 0.0 copy-start.3
  73.0 0.0 copy-start.4
  73.0 2.4 broadcast_in_dim.74
  75.4 0.0 copy-done.3
  75.4 0.0 copy-done.4
  75.4 17.4 %while.26 = (s32[]{:T(128)}, f32[32,128,256]{2,1,0:T(8,128)}, s32[32]{0:T(128)S(1)}, bf16[32,128,128]{2,1,0:T(8,128)(2,1)}, s32[32]{0:T(128)S(1)}, /*index=5*/bf...) while((s32[]{:T(128)}, f32[32,128,256]{2,1,0:T(8,128)}, ...), condition=%wide.region_2.3_spmd, body=%wide.region_0.2_spmd.sunk | while | flops 135791808 | bytes 12063503 | solution.py:42
  75.4 0.7 compare_and_fusion.4
  76.1 1.8 gather_fusion
  78.0 1.5 convolution_multiply_fusion.4
  79.5 0.1 compare_select_fusion.8
  79.6 4.4 scatter_fusion
  84.1 0.7 compare_and_fusion.4
  84.8 1.8 gather_fusion
  86.6 1.5 convolution_multiply_fusion.4
  88.2 0.1 compare_select_fusion.8
  88.3 4.5 scatter_fusion
  92.8 3.8 convert_element_type.46
  96.6 0.0 copy-start.5
  96.6 0.0 copy-start.1
  96.6 0.0 reduce-scatter.3.cloned.1.call-update
  96.6 0.0 all-gather.5.cloned.1.call-start
  96.7 107.9 %reduce-scatter.3.cloned.1.call-done = bf16[128,256]{1,0:T(8,128)(2,1)} async-done(((bf16[4096,256]{1,0:T(8,128)(2,1)}), bf16[128,256]{1,0:T(8,128)(2,1)}) %reduce-scatter.3.cloned.1.call-update) | async-done | bytes 65552 | tf_op jit(solution)/shard_map/reduce_scatter | solution.py:60
  204.6 0.0 copy-done
  204.6 0.0 copy-done.5
  204.6 0.0 copy-start.2
  204.6 1.8 multiply_convert_fusion
  206.4 0.8 convolution_convert_fusion
  207.2 0.0 all-gather.5.cloned.1.call-update
  207.2 0.0 all-reduce.2.cloned.1.call-start
  207.3 0.0 copy-done.1
  207.3 1.3 copy.10
  208.6 0.0 copy-done.2
  208.6 0.9 fusion.12
  209.5 0.0 all-reduce.2.cloned.1.call-update
  209.5 0.0 reduce-scatter.5.cloned.1.call-start
  209.6 70.9 %all-gather.5.cloned.1.call-done = bf16[4096,256]{1,0:T(8,128)(2,1)} async-done(((bf16[128,256]{1,0:T(8,128)(2,1)}), bf16[4096,256]{1,0:T(8,128)(2,1)}) %all-gather.5.cloned.1.call-update) | async-done | bytes 2097168 | tf_op jit(solution)/shard_map/all_gather | solution.py:75
  280.5 1.5 broadcast_in_dim.75
  282.0 18.0 %while.27 = (s32[]{:T(128)}, f32[16,128,256]{2,1,0:T(8,128)}, s32[32]{0:T(128)S(1)}, bf16[32,128,128]{1,2,0:T(8,128)(2,1)}, s32[32]{0:T(128)S(1)}, /*index=5*/bf...) while((s32[]{:T(128)}, f32[16,128,256]{2,1,0:T(8,128)}, ...), condition=%wide.region_6.7_spmd, body=%wide.region_4.6_spmd.sunk | while | flops 135791808 | bytes 12063503 | solution.py:42
  282.0 0.7 compare_and_fusion.5
  282.8 2.2 gather_fusion.1
  285.0 1.5 convolution_multiply_fusion.5
  286.5 0.1 compare_select_fusion.9
  286.6 4.4 scatter_fusion.1
  291.0 0.7 compare_and_fusion.5
  291.8 2.2 gather_fusion.1
  294.0 1.5 convolution_multiply_fusion.5
  295.5 0.1 compare_select_fusion.9
  295.6 4.4 scatter_fusion.1
  300.0 2.7 convert_element_type.52
  302.7 0.0 reduce-scatter.5.cloned.1.call-update
  302.7 437.0 %all-reduce.2.cloned.1.call-done = f32[256,256]{1,0:T(8,128)} async-done(((f32[256,256]{1,0:T(8,128)}), f32[256,256]{1,0:T(8,128)}) %all-reduce.2.cloned.1.call-update) | async-done | bytes 262160 | tf_op jit(solution)/shard_map/psum | solution.py:71
  739.7 1.7 broadcast_multiply_fusion
  741.4 86.6 %reduce-scatter.5.cloned.1.call-done = bf16[128,256]{1,0:T(8,128)(2,1)} async-done(((bf16[2048,256]{1,0:T(8,128)(2,1)}), bf16[128,256]{1,0:T(8,128)(2,1)}) %reduce-scatter.5.cloned.1.call-update) | async-done | bytes 65552 | tf_op jit(solution)/shard_map/reduce_scatter | solution.py:81
  (4 shorter events, 0.0 us)
Async XLA Ops:
  7.2 197.4 %copy-start = (bf16[256,256]{1,0:T(8,128)(2,1)S(1)}, bf16[256,256]{1,0:T(8,128)(2,1)}, u32[]{:S(2)}) copy-start(bf16[256,256]{1,0:T(8,128)(2,1)} %param.12) | copy-start | bytes 393220
  7.2 65.8 %all-gather.3.cloned.1.call-start = ((), (), s32[]{:S(2)}) async-start(), calls=%async_computation.2 | async-start | bytes 1114112 | tf_op jit(solution)/shard_map/all_gather | solution.py:54
  7.9 196.7 %reduce-scatter.3.cloned.1.call-start = ((), (), s32[]{:S(2)}) async-start(), calls=%async_computation.3 | async-start | bytes 2162688 | tf_op jit(solution)/shard_map/reduce_scatter | solution.py:60
  73.0 2.5 copy-start.3
  73.0 2.5 copy-start.4
  96.6 108.0 %copy-start.5 = (bf16[128,256]{1,0:T(8,128)(2,1)S(1)}, bf16[128,256]{1,0:T(8,128)(2,1)}, u32[]{:S(2)}) copy-start(bf16[128,256]{1,0:T(8,128)(2,1)} %param.17) | copy-start | bytes 196612
  96.6 110.7 %copy-start.1 = (bf16[32,128,128]{2,1,0:T(8,128)(2,1)S(1)}, bf16[32,128,128]{2,1,0:T(8,128)(2,1)}, u32[]{:S(2)}) copy-start(bf16[32,128,128]{2,1,0:T(8,128)(2,1)} %get-tuple-element.465) | copy-start | bytes 3145732
  96.6 183.9 %all-gather.5.cloned.1.call-start = ((), (), s32[]{:S(2)}) async-start(), calls=%async_computation.4 | async-start | bytes 2162688 | tf_op jit(solution)/shard_map/all_gather | solution.py:75
  204.6 4.0 copy-start.2
  207.2 532.5 %all-reduce.2.cloned.1.call-start = ((), (), s32[]{:S(2)}) async-start(), calls=%async_computation.6 | async-start | bytes 524288 | tf_op jit(solution)/shard_map/psum | solution.py:71
  209.5 618.4 %reduce-scatter.5.cloned.1.call-start = ((), (), s32[]{:S(2)}) async-start(), calls=%async_computation.5 | async-start | bytes 1114112 | tf_op jit(solution)/shard_map/reduce_scatter | solution.py:81
Sparse Core Ops, SparseCore 0:
  11.0 61.8 all-gather.2
  96.7 107.8 reduce-scatter.2
  207.5 72.9 all-gather.4
  287.3 452.4 all-reduce.1
  744.2 83.6 reduce-scatter.4
where the time goes:
time: 836 us; the launch traced here: 834 us
  waiting for transfers between devices  768 us (92%)
  other arithmetic  29.1 us (3%)
  between operations  13.8 us (2%)
  local copies, waits for them, and re-layouts  13.4 us (2%)
  matrix products  9.69 us (1%)
    psum x1, waiting for transfers between devices, on_device(): weight_grad = lax.psum(local_grad, ('row', 'col')) * scaling  437 us
    reduce_scatter x1, waiting for transfers between devices, on_device(): lax.psum_scatter(partial_value.astype(jnp.bfloat16), 'col', scatter_dimen...  108 us
    reduce_scatter x1, waiting for transfers between devices, on_device(): lax.psum_scatter(back_terms.astype(jnp.bfloat16), 'row', scatter_dimensio...  86.6 us
    all_gather x1, waiting for transfers between devices, on_device(): grad_block = lax.all_gather(aggregate_grad, 'col', axis=0, tiled=True)  70.9 us
    all_gather x1, waiting for transfers between devices, on_device(): panel = lax.all_gather(features, 'row', axis=0, tiled=True)  65 us
    scatter-add x4, other arithmetic, block_terms(): return total.at[target].add(products * active[:, None, None])  17.7 us
  transfers between devices with their start and end apart: 5, of which 5 were waited for; matrix products, arithmetic and copies ran while one was open for 3% of the time, Pallas kernels for 0%

commit v1 on v0

v1 whole, which is shorter than its diff:
```python
import functools
import math

import jax
import jax.numpy as jnp
from jax import lax
from jax.experimental import pallas as pl
from jax.experimental.pallas import tpu as pltpu
from jax.sharding import PartitionSpec as P

MESH = pl.DeviceIdType.MESH
BF = jnp.bfloat16
F32 = jnp.float32
NX, NY, NZ, NR = 4, 4, 16, 16
SLOTS, ROW_T, COL_T, T = 32, 32, 16, 128
H = 128


def remote(src, dst, send, recv, device):
    return pltpu.make_async_remote_copy(
        src_ref=src, dst_ref=dst, send_sem=send, recv_sem=recv, device_id=device, device_id_type=MESH
    )


def slot_tables(rows, cols, count, table):
    sub = lax.broadcasted_iota(jnp.int32, (SLOTS, SLOTS), 0)
    lane = lax.broadcasted_iota(jnp.int32, (SLOTS, SLOTS), 1)
    used = sub < count[...]

    def latest(mask):
        found = jnp.max(jnp.where(mask, sub, -1), axis=0, keepdims=True)
        return jnp.where(found < 0, SLOTS, found)

    for base, ref in ((0, rows), (2, cols)):
        along = jnp.broadcast_to(ref[...], (SLOTS, SLOTS))
        down = jnp.sum(jnp.where(sub == lane, along, 0), axis=1, keepdims=True)
        table[base : base + 1, :SLOTS] = latest((down == along) & (sub < lane) & used)
        table[base + 1 : base + 2, :SLOTS] = latest((down == lane) & used)
        table[4 + base // 2 : 5 + base // 2, :SLOTS] = ref[...]


def kernel(
    feat, weight, vals, rows, cols, count, cot, out, fgrad, wgrad,
    table, idx, panel, acc, pair_out, pair_in, own_out, own_in, first, chain, side_in,
    grads, back_out, back_in, w_loc, w_pair, w_sum, w_x, w_z, w_all, w_other,
    idx_sem, g_send, g_recv, p_send, p_recv, o_send, o_recv, c_send, c_recv, f_send, f_recv,
    a_send, a_recv, q_send, q_recv, b_send, b_recv, wp_send, wp_recv, wx_send, wx_recv,
    wz_send, wz_recv, wa_send, wa_recv, wo_send, wo_recv,
):
    r, c = lax.axis_index("row"), lax.axis_index("col")
    z, k = lax.div(c, 2), lax.rem(c, 2)
    sigma = 1 - 2 * k
    partner = (r, 2 * z + 1 - k)

    def at_row(d):
        return (lax.rem(r + d, NR), c)

    def at_z(d):
        return (r, 2 * lax.rem(z + d + 2 * NZ, NZ) + k)

    def chip(d):
        return lax.rem(z + sigma * d + NZ, NZ)

    ahead = (r, 2 * chip(1) + k)

    barrier = pltpu.get_barrier_semaphore()

    def greet(d, carry):
        pl.semaphore_signal(barrier, inc=1, device_id=at_row(d), device_id_type=MESH)
        pl.semaphore_signal(barrier, inc=1, device_id=at_z(d), device_id_type=MESH)
        return carry

    lax.fori_loop(1, NR, greet, 0)
    pl.semaphore_signal(barrier, inc=1, device_id=partner, device_id_type=MESH)
    slot_tables(rows, cols, count, table)
    to_idx = pltpu.make_async_copy(table, idx, idx_sem)
    to_idx.start()
    panel[r] = feat[...]
    acc[SLOTS] = jnp.zeros((2, T, H), F32)
    pl.semaphore_wait(barrier, 2 * (NR - 1) + 1)

    def gather(d):
        return remote(feat, panel.at[r], g_send.at[d], g_recv.at[d], at_row(d))

    def gather_from(d):
        return remote(
            feat, panel.at[lax.rem(r - d + NR, NR)], g_send.at[d], g_recv.at[d], at_row(d)
        )

    lax.fori_loop(1, NR, lambda d, u: (gather(d).start(), u)[1], 0)
    to_idx.wait()
    lax.fori_loop(1, NR, lambda d, u: (gather_from(d).wait_recv(), u)[1], 0)

    def add_forward(i, carry):
        for j in range(4):
            s = 4 * i + j
            product = jnp.dot(vals[s], panel[idx[5, s]], preferred_element_type=F32)
            before = idx[0, s]
            for h in range(2):
                acc[s, h] = acc[before, h] + product[:, h * H : (h + 1) * H]
        return carry

    lax.fori_loop(0, SLOTS // 4, add_forward, 0)

    def pair(d):
        return remote(pair_out.at[d], pair_in.at[d], p_send.at[d], p_recv.at[d], partner)

    def hand_over(i, carry):
        d = 8 - i
        for ct in range(2):
            last = idx[1, 2 * chip(-d) + ct]
            for h in range(2):
                pair_out[d, ct, h] = acc[last, h].astype(BF)
        pair(d).start()
        return carry

    lax.fori_loop(0, 8, hand_over, 0)
    theirs = idx[1, 2 * z + 1 - k]
    for h in range(2):
        own_out[h] = acc[theirs, h].astype(BF)
    own_copy = remote(own_out, own_in, o_send, o_recv, partner)
    own_copy.start()

    def link(s, ct, h):
        return remote(
            chain.at[s - 1, ct, h], chain.at[s, ct, h], c_send.at[s, ct, h], c_recv.at[s, ct, h], ahead
        )

    pair(8).wait_recv()
    starts = [
        remote(first.at[ct], chain.at[1, ct, k], f_send.at[ct], c_recv.at[1, ct, k], ahead)
        for ct in range(2)
    ]
    for ct in range(2):
        last = idx[1, 2 * chip(8) + ct]
        first[ct] = (acc[last, k] + pair_in[8, ct, k].astype(F32)).astype(BF)
        starts[ct].start()

    pair(7).wait_recv()
    for ct in range(2):
        last = idx[1, 2 * chip(7) + ct]
        chain[1, ct, 1 - k] = (acc[last, 1 - k] + pair_in[7, ct, 1 - k].astype(F32)).astype(BF)
        link(2, ct, 1 - k).start()
    for ct in range(2):
        last = idx[1, 2 * chip(7) + ct]
        starts[ct].wait_recv()
        chain[1, ct, k] = (
            acc[last, k] + pair_in[7, ct, k].astype(F32) + chain[1, ct, k].astype(F32)
        ).astype(BF)
        link(2, ct, k).start()

    def pass_on(s, carry):
        d = 9 - s
        pair(d).wait_recv()
        for h in range(2):
            for ct in range(2):
                last = idx[1, 2 * chip(d) + ct]
                link(s - 1, ct, h).wait_recv()
                chain[s - 1, ct, h] = (
                    acc[last, h] + pair_in[d, ct, h].astype(F32) + chain[s - 1, ct, h].astype(F32)
                ).astype(BF)
                link(s, ct, h).start()
        return carry

    lax.fori_loop(3, 9, pass_on, 0)

    def side(h):
        return remote(chain.at[8, 1 - k, h], side_in.at[h], f_send.at[2 + h], f_recv.at[h], partner)

    for h in range(2):
        link(8, 1 - k, h).wait_recv()
        side(h).start()
    own_copy.wait_recv()
    mine = idx[1, 2 * z + k]
    halves = []
    for h in range(2):
        link(8, k, h).wait_recv()
        halves.append(acc[mine, h] + own_in[h].astype(F32) + chain[8, k, h].astype(F32))
    for h in range(2):
        side(h).wait_recv()
        halves[h] = (halves[h] + side_in[h].astype(F32)).astype(BF)
    aggregated = jnp.concatenate(halves, axis=1)

    preact = jnp.dot(aggregated, weight[...], preferred_element_type=F32)
    logistic = jax.nn.sigmoid(preact)
    pre_grad = (cot[...].astype(F32) * logistic * (1.0 + preact * (1.0 - logistic))).astype(BF)
    aggregate_grad = lax.dot_general(
        pre_grad, weight[...], (((1,), (1,)), ((), ())), preferred_element_type=F32
    ).astype(BF)

    for h in range(2):
        grads[z, k, h] = aggregate_grad[:, h * H : (h + 1) * H]

    def onward(s, ct, h):
        tile = grads.at[chip(1 - s), ct, h]
        return remote(tile, tile, a_send.at[s, ct, h], a_recv.at[s, ct, h], ahead)

    def arrival(s, ct, h):
        tile = grads.at[chip(-s), ct, h]
        return remote(tile, tile, a_send.at[s, ct, h], a_recv.at[s, ct, h], ahead)

    twin = remote(grads.at[z, k], grads.at[z, k], q_send.at[0, 0], q_recv.at[0, 0], partner)
    twin_in = remote(grads.at[z, 1 - k], grads.at[z, 1 - k], q_send.at[0, 0], q_recv.at[0, 0], partner)
    twin.start()
    for h in range(2):
        onward(1, k, h).start()
    out[...] = (preact * logistic).astype(BF)
    local_grad = lax.dot_general(
        aggregated, pre_grad, (((0,), (0,)), ((), ())), preferred_element_type=F32
    )
    w_loc[...] = local_grad
    for q in range(2):
        for p in range(NR):
            at = q * 128 + (p // 2) * 16
            w_sum[q, p] = w_loc[at : at + 16, (p % 2) * H : (p % 2 + 1) * H].astype(BF)
    twin_in.wait_recv()
    for h in range(2):
        onward(1, 1 - k, h).start()
    w_swap = remote(w_sum.at[1 - k], w_pair, wp_send, wp_recv, partner)
    w_swap.start()

    def both(s):
        there, here = grads.at[chip(-s)], grads.at[chip(s)]
        return (
            remote(there, there, q_send.at[s, 0], q_recv.at[s, 0], partner),
            remote(here, here, q_send.at[s, 0], q_recv.at[s, 0], partner),
        )

    def far(ct):
        there, here = grads.at[chip(8), ct, k], grads.at[chip(8), ct, 1 - k]
        return (
            remote(there, there, q_send.at[8, ct], q_recv.at[8, ct], partner),
            remote(here, here, q_send.at[8, ct], q_recv.at[8, ct], partner),
        )

    def advance(s):
        for ct in (k, 1 - k):
            for h in range(2):
                arrival(s, ct, h).wait_recv()
                if s < 7:
                    onward(s + 1, ct, h).start()
            if s == 7:
                onward(8, ct, k).start()
        both(s)[0].start()

    def w_spread(d):
        return remote(
            w_sum.at[k, lax.rem(r + d, NR)], w_x.at[d], wx_send.at[d], wx_recv.at[d], at_row(d)
        )

    def w_along(d):
        return remote(w_z.at[z], w_z.at[z], wz_send.at[d], wz_recv.at[d], at_z(d))

    def w_along_in(d):
        there = w_z.at[lax.rem(z - d + NZ, NZ)]
        return remote(there, there, wz_send.at[d], wz_recv.at[d], at_z(d))

    def w_share(d):
        return remote(w_all.at[r], w_all.at[r], wa_send.at[d], wa_recv.at[d], at_row(d))

    def w_share_in(d):
        there = w_all.at[lax.rem(r - d + NR, NR)]
        return remote(there, there, wa_send.at[d], wa_recv.at[d], at_row(d))

    def each(make, act):
        lax.fori_loop(1, NR, lambda d, u: (act(make(d)), u)[1], 0)

    def start(copy):
        copy.start()

    def landed(copy):
        copy.wait_recv()

    def sent(copy):
        copy.wait_send()

    advance(1)
    w_swap.wait()
    w_sum[k] = (w_sum[k].astype(F32) + w_pair[...].astype(F32)).astype(BF)
    each(w_spread, start)
    advance(2)
    advance(3)
    each(w_spread, landed)
    part = lax.fori_loop(
        1, NR, lambda d, total: total + w_x[d].astype(F32), w_sum[k, r].astype(F32)
    )
    w_z[z] = part.astype(BF)
    each(w_along, start)
    advance(4)
    advance(5)
    advance(6)
    each(w_along_in, landed)
    whole = lax.fori_loop(
        1, NZ, lambda i, total: total + w_z[i].astype(F32), w_z[0].astype(F32)
    )
    w_all[r] = whole * (1.0 / math.sqrt(NR * 2 * NZ * T))
    each(w_share, start)
    advance(7)
    for ct in range(2):
        arrival(8, ct, k).wait_recv()
        far(ct)[0].start()
    for s in range(1, 8):
        both(s)[1].wait_recv()
    for ct in range(2):
        far(ct)[1].wait_recv()

    def add_backward(i, carry):
        for j in range(4):
            s = 4 * i + j
            row = idx[4, s]
            top, ct = lax.div(row, 2), lax.rem(row, 2)
            tile = jnp.concatenate([grads[top, ct, 0], grads[top, ct, 1]], axis=1)
            product = lax.dot_general(
                vals[s], tile, (((0,), (0,)), ((), ())), preferred_element_type=F32
            )
            before = idx[2, s]
            for h in range(2):
                acc[s, h] = acc[before, h] + product[:, h * H : (h + 1) * H]
        return carry

    lax.fori_loop(0, SLOTS // 4, add_backward, 0)

    def back(d):
        return remote(back_out.at[d], back_in.at[d], b_send.at[d], b_recv.at[d], at_row(d))

    def give_back(d, carry):
        last = idx[3, lax.rem(r + d, NR)]
        for h in range(2):
            back_out[d, :, h * H : (h + 1) * H] = acc[last, h].astype(BF)
        back(d).start()
        return carry

    lax.fori_loop(1, NR, give_back, 0)

    each(w_share_in, landed)
    w_far = remote(w_all, w_other, wo_send, wo_recv, partner)
    w_far.start()
    for p in range(NR):
        at = pl.multiple_of(k * 128 + (p // 2) * 16, 16)
        wgrad[pl.ds(at, 16), (p % 2) * H : (p % 2 + 1) * H] = w_all[p]
    w_far.wait_recv()
    for p in range(NR):
        at = pl.multiple_of((1 - k) * 128 + (p // 2) * 16, 16)
        wgrad[pl.ds(at, 16), (p % 2) * H : (p % 2 + 1) * H] = w_other[p]

    each(gather, sent)
    for d in range(1, 9):
        pair(d).wait_send()
    own_copy.wait_send()
    for ct in range(2):
        starts[ct].wait_send()
        side(ct).wait_send()
        far(ct)[0].wait_send()
        onward(8, ct, k).wait_send()
    for s in range(1, 8):
        both(s)[0].wait_send()
        for ct in range(2):
            for h in range(2):
                link(s + 1, ct, h).wait_send()
                onward(s, ct, h).wait_send()
    twin.wait_send()
    each(w_spread, sent)
    each(w_along, sent)
    each(w_share, sent)
    w_far.wait_send()

    each(back, landed)
    last = idx[3, r]
    for h in range(2):
        cut = slice(h * H, (h + 1) * H)
        total = lax.fori_loop(
            1, NR, lambda d, total: total + back_in[d, :, cut].astype(F32), acc[last, h]
        )
        fgrad[:, cut] = total.astype(BF)
    each(back, sent)


def on_device(features, weight, tile_values, tile_rows, tile_cols, tile_count, cotangent):
    width = features.shape[1]
    dma = pltpu.SemaphoreType.DMA
    vmem = pltpu.VMEM
    return pl.pallas_call(
        kernel,
        out_shape=(
            jax.ShapeDtypeStruct((T, width), BF),
            jax.ShapeDtypeStruct((T, width), BF),
            jax.ShapeDtypeStruct((width, width), F32),
        ),
        in_specs=[pl.BlockSpec(memory_space=pltpu.VMEM)] * 7,
        out_specs=(pl.BlockSpec(memory_space=pltpu.VMEM),) * 3,
        scratch_shapes=[
            vmem((8, 128), jnp.int32),
            pltpu.SMEM((8, 128), jnp.int32),
            vmem((COL_T, T, width), BF),
            vmem((SLOTS + 1, 2, T, H), F32),
            vmem((9, 2, 2, T, H), BF),
            vmem((9, 2, 2, T, H), BF),
            vmem((2, T, H), BF),
            vmem((2, T, H), BF),
            vmem((2, T, H), BF),
            vmem((9, 2, 2, T, H), BF),
            vmem((2, T, H), BF),
            vmem((NZ, 2, 2, T, H), BF),
            vmem((NR, T, width), BF),
            vmem((NR, T, width), BF),
            vmem((width, width), F32),
            vmem((NR, 16, 128), BF),
            vmem((2, NR, 16, 128), BF),
            vmem((NR, 16, 128), BF),
            vmem((NZ, 16, 128), BF),
            vmem((NR, 16, 128), F32),
            vmem((NR, 16, 128), F32),
            dma,
            dma((NR,)), dma((NR,)),
            dma((9,)), dma((9,)),
            dma, dma,
            dma((9, 2, 2)), dma((9, 2, 2)),
            dma((4,)), dma((2,)),
            dma((9, 2, 2)), dma((9, 2, 2)),
            dma((9, 2)), dma((9, 2)),
            dma((NR,)), dma((NR,)),
            dma, dma,
            dma((NR,)), dma((NR,)),
            dma((NZ,)), dma((NZ,)),
            dma((NR,)), dma((NR,)),
            dma, dma,
        ],
        compiler_params=pltpu.CompilerParams(
            collective_id=0, has_side_effects=True, vmem_limit_bytes=48 * 2**20
        ),
    )(
        features,
        weight,
        tile_values.reshape(SLOTS, T, T),
        tile_rows.reshape(1, SLOTS),
        tile_cols.reshape(1, SLOTS),
        tile_count.reshape(1, 1),
        cotangent,
    )


def solution(mesh):
    return jax.shard_map(
        on_device,
        mesh=mesh,
        in_specs=(
            P(("col", "row"), None),
            P(),
            P("row", "col", None, None, None),
            P("row", "col", None),
            P("row", "col", None),
            P("row", "col"),
            P(("row", "col"), None),
        ),
        out_specs=(P(("row", "col"), None), P(("col", "row"), None), P()),
        check_vma=False,
    )
```

time: 836 us -> 120 us (0.14)
  waiting for transfers between devices: 768 us -> 0 us
  Pallas kernels: 0 us -> 111 us
  other arithmetic: 29.1 us -> 0 us
  between operations: 13.8 us -> 1.31 us
  matrix products: 9.69 us -> 0 us
    psum x1 -> x0, waiting for transfers between devices: 437 us -> none  [on_device(): weight_grad = lax.psum(local_grad, ('row', 'col')) * scaling]
    reduce_scatter x2 -> x0, waiting for transfers between devices: 195 us -> none  [the longest x1 108 us: on_device(): lax.psum_scatter(partial_value.astype(jnp.bfloat16), 'col', scatter_dimen...]
    all_gather x2 -> x0, waiting for transfers between devices: 136 us -> none  [the longest x1 70.9 us: on_device(): grad_block = lax.all_gather(aggregate_grad, 'col', axis=0, tiled=True)]
    pallas_call x0 -> x1, Pallas kernels: none -> 111 us  [on_device(): pl.pallas_call(kernel, out_shape=(jax.ShapeDtypeStruct((T, width), BF), j...]
    scatter-add x4 -> x0, other arithmetic: 17.7 us -> none  [block_terms(): return total.at[target].add(products * active[:, None, None])]
    dot_general x7 -> x0, matrix products: 9.69 us -> none  [the longest x4 6.2 us: block_terms(): jnp.einsum(form, values, picked, preferred_element_type=jnp.float32)]
  transfers between devices with their start and end apart: 5 -> 0, of which waited for: 5 -> 0; matrix products, arithmetic and copies ran while one was open for 3% -> 0% of each run, Pallas kernels for 0% -> 0%
where the time goes in v1:
time: 120 us; the launch traced here: 119 us
  Pallas kernels  111 us (92%)
  local copies, waits for them, and re-layouts  6.42 us (5%)
  between operations  1.31 us (1%)
    pallas_call x1, Pallas kernels, on_device(): pl.pallas_call(kernel, out_shape=(jax.ShapeDtypeStruct((T, width), BF), j...  111 us
    unnamed x15, local copies, waits for them, and re-layouts  6.42 us

profile of v1, /device:TPU:1, one launch (start us, length us, event | category | flops | bytes accessed | tf_op | source)
XLA Modules:
  0.0 118.8 jit_solution(8049579967534570475)
XLA Ops:
  1.3 0.0 copy-start.4
  1.3 0.0 copy-start.5
  1.3 0.6 copy-done.4
  1.9 0.0 copy-done.5
  2.0 0.0 copy-start
  2.0 1.2 %copy-done = bf16[1,1,32,128,128]{4,3,2,1,0:T(8,128)(2,1)S(1)} copy-done((bf16[1,1,32,128,128]{4,3,2,1,0:T(8,128)(2,1)S(1)}, bf16[1,1,32,128,128]{4,3,2,1,0:T(8,128)(2,1)}, u32[]{:S(2)}) %copy-start) | copy-done | bytes 1048600
  3.2 0.0 copy-start.1
  3.2 0.9 copy-done.1
  4.1 0.0 copy-start.2
  4.1 0.8 copy-done.2
  4.9 0.0 copy-start.3
  4.9 0.8 copy-done.3
  5.8 111.0 %shard_map.94 = (bf16[128,256]{1,0:T(8,128)(2,1)S(1)}, bf16[128,256]{1,0:T(8,128)(2,1)S(1)}, f32[256,256]{1,0:T(8,128)S(1)}) custom-call(bf16[128,256]{1,0:T(8,128)(2,1)S(1)} %copy-done.2, bf16[256,256]{1,0:T(8,128)(2,1)S(1)} %copy-done.1, bf16[32,128,128]{2,1,0:T(8,128)(2,1)S(1)} %bitcast.3, s32[1,32]{1,0:T(1,128)S(1)} %bitcast.4, s32[1,32]{1,0:T(1,128)S(1)} %bitcast.5, ...), custom_call_target="tpu_custom_call" | custom-call | tf_op jit(solution)/shard_map/pallas_call | solution.py:382
  116.8 0.6 copy.14
  117.4 0.6 copy.15
  118.1 0.7 copy.16
Async XLA Ops:
  1.3 0.7 copy-start.4
  1.3 0.7 copy-start.5
  2.0 1.2 %copy-start = (bf16[1,1,32,128,128]{4,3,2,1,0:T(8,128)(2,1)S(1)}, bf16[1,1,32,128,128]{4,3,2,1,0:T(8,128)(2,1)}, u32[]{:S(2)}) copy-start(bf16[1,1,32,128,128]{4,3,2,1,0:T(8,128)(2,1)} %param.9) | copy-start | bytes 3145732
  3.2 0.9 copy-start.1
  4.1 0.8 copy-start.2
  4.9 0.8 copy-start.3

commit v2 on v0

v2 whole, which is shorter than its diff:
```python
import functools
import math

import jax
import jax.numpy as jnp
from jax import lax
from jax.experimental import pallas as pl
from jax.experimental.pallas import tpu as pltpu
from jax.sharding import PartitionSpec as P

MESH = pl.DeviceIdType.MESH
BF = jnp.bfloat16
F32 = jnp.float32
NX, NY, NZ, NR = 4, 4, 16, 16
SLOTS, ROW_T, COL_T, T = 32, 32, 16, 128
H = 128


def remote(src, dst, send, recv, device):
    return pltpu.make_async_remote_copy(
        src_ref=src, dst_ref=dst, send_sem=send, recv_sem=recv, device_id=device, device_id_type=MESH
    )


def slot_tables(rows, cols, count, table):
    sub = lax.broadcasted_iota(jnp.int32, (SLOTS, SLOTS), 0)
    lane = lax.broadcasted_iota(jnp.int32, (SLOTS, SLOTS), 1)
    used = sub < count

    def latest(mask):
        found = jnp.max(jnp.where(mask, sub, -1), axis=0, keepdims=True)
        return jnp.where(found < 0, SLOTS, found)

    for base, ref in ((0, rows), (2, cols)):
        along = jnp.broadcast_to(ref[...], (SLOTS, SLOTS))
        down = jnp.sum(jnp.where(sub == lane, along, 0), axis=1, keepdims=True)
        table[base : base + 1, :SLOTS] = latest((down == along) & (sub < lane) & used)
        table[base + 1 : base + 2, :SLOTS] = latest((down == lane) & used)
        table[4 + base // 2 : 5 + base // 2, :SLOTS] = ref[...]


def kernel(
    feat, weight_hbm, vals_hbm, rows_hbm, cols_hbm, count, cot_hbm, out, fgrad, wgrad,
    weight, vals, rows, cols, cot, table, idx, panel_a, panel_b, acc, pair_out, pair_in, own_out, own_in, first, leaf_out,
    chain_in, leaf_in, side_out, side_in, grads_a, grads_b, back_out, back_in,
    w_loc, w_pair, w_sum, w_x, w_z, w_all, w_other,
    in_sem, idx_sem, g_send, g_recv, p_send, p_recv, o_send, o_recv, c_send, c_recv, l_send, l_recv, f_send, f_recv,
    a_send, a_recv, al_send, al_recv, q_send, q_recv, ql_send, ql_recv, t_send, t_recv, b_send, b_recv,
    wp_send, wp_recv, wx_send, wx_recv, wz_send, wz_recv, wa_send, wa_recv, wo_send, wo_recv,
):
    panel, grads = (panel_a, panel_b), (grads_a, grads_b)
    r, c = lax.axis_index("row"), lax.axis_index("col")
    z, k = lax.div(c, 2), lax.rem(c, 2)
    other = 1 - k
    sigma = 1 - 2 * k
    partner = (r, 2 * z + other)

    def at_row(d):
        return (lax.rem(r + d, NR), c)

    def at_z(d):
        return (r, 2 * lax.rem(z + d, NZ) + k)

    chips = {d: lax.rem(z + sigma * d + NZ, NZ) for d in range(-8, 9)}
    one, two = (r, 2 * chips[1] + k), (r, 2 * chips[2] + k)
    sent = []

    def start(copy):
        copy.start()
        sent.append(copy)

    def each(make, act):
        lax.fori_loop(1, NR, lambda d, u: (act(make(d)), u)[1], 0)

    def begin(copy):
        copy.start()

    def landed(copy):
        copy.wait_recv()

    def gone(copy):
        copy.wait_send()

    loads = [
        pltpu.make_async_copy(rows_hbm, rows, in_sem.at[0]),
        pltpu.make_async_copy(cols_hbm, cols, in_sem.at[1]),
        pltpu.make_async_copy(feat.at[:, 0:H], panel[0].at[r], in_sem.at[2]),
        pltpu.make_async_copy(feat.at[:, H : 2 * H], panel[1].at[r], in_sem.at[3]),
        pltpu.make_async_copy(vals_hbm, vals, in_sem.at[4]),
        pltpu.make_async_copy(weight_hbm, weight, in_sem.at[5]),
        pltpu.make_async_copy(cot_hbm, cot, in_sem.at[6]),
    ]
    for load in loads:
        load.start()
    barrier = pltpu.get_barrier_semaphore()

    def greet(d, carry):
        pl.semaphore_signal(barrier, inc=1, device_id=at_z(d), device_id_type=MESH)
        pl.semaphore_signal(barrier, inc=1, device_id=at_row(d), device_id_type=MESH)
        return carry

    lax.fori_loop(1, NR, greet, 0)
    pl.semaphore_signal(barrier, inc=1, device_id=partner, device_id_type=MESH)
    for h in range(2):
        acc[h, SLOTS] = jnp.zeros((T, H), F32)
    loads[0].wait()
    loads[1].wait()
    slot_tables(rows, cols, count[0, 0], table)
    to_idx = pltpu.make_async_copy(table, idx, idx_sem)
    to_idx.start()
    for load in loads[2:]:
        load.wait()
    to_idx.wait()
    pl.semaphore_wait(barrier, 2 * (NR - 1) + 1)

    def gather(h):
        mine = panel[h].at[r]
        return lambda d: remote(mine, mine, g_send.at[h, d], g_recv.at[h, d], at_row(d))

    def gathered(h):
        def make(d):
            theirs = panel[h].at[lax.rem(r - d + NR, NR)]
            return remote(theirs, theirs, g_send.at[h, d], g_recv.at[h, d], at_row(d))

        return make

    for h in range(2):
        each(gather(h), begin)

    def forward(h):
        each(gathered(h), landed)

        def step(i, carry):
            for j in range(8):
                s = 8 * i + j
                acc[h, s] = acc[h, idx[0, s]] + jnp.dot(
                    vals[s], panel[h][idx[5, s]], preferred_element_type=F32
                )
            return carry

        lax.fori_loop(0, SLOTS // 8, step, 0)

    def pair(h, g):
        return remote(pair_out.at[h, g], pair_in.at[h, g], p_send.at[h, g], p_recv.at[h, g], partner)

    def own_copy(h):
        return remote(own_out.at[h], own_in.at[h], o_send.at[h], o_recv.at[h], partner)

    def hand_over(h):
        for g in range(4):
            for j in range(2):
                for ct in range(2):
                    last = idx[1, 2 * chips[2 * g + j - 8] + ct]
                    pair_out[h, g, j, ct] = acc[h, last].astype(BF)
            start(pair(h, g))
        own_out[h] = acc[h, idx[1, 2 * z + other]].astype(BF)
        start(own_copy(h))

    def both(h, d, ct):
        last = idx[1, 2 * chips[d] + ct]
        return acc[h, last] + pair_in[h, (8 - d) // 2, (8 - d) % 2, ct].astype(F32)

    def link(h, s, ct):
        source = first.at[h] if s == 1 else chain_in.at[h, s - 2, ct]
        return remote(
            source, chain_in.at[h, s - 1, ct], c_send.at[h, s - 1, ct], c_recv.at[h, s - 1, ct], two
        )

    def leaf(h, i):
        return remote(leaf_out.at[h, i], leaf_in.at[h, i], l_send.at[h, i], l_recv.at[h, i], one)

    def send_leaf(h, i):
        for ct in range(2):
            leaf_out[h, i, ct] = both(h, 7 - 2 * i, ct).astype(BF)
        start(leaf(h, i))

    def sums_begin(h):
        pair(h, 0).wait_recv()
        first[h] = both(h, 8, k).astype(BF)
        start(link(h, 1, k))
        send_leaf(h, 0)

    def sums_step(h, s):
        pair(h, s - 1).wait_recv()
        leaf(h, s - 2).wait_recv()
        for ct in (other, k):
            total = both(h, 10 - 2 * s, ct) + leaf_in[h, s - 2, ct].astype(F32)
            if s > 2 or ct is k:
                link(h, s - 1, ct).wait_recv()
                total = total + chain_in[h, s - 2, ct].astype(F32)
            chain_in[h, s - 2, ct] = total.astype(BF)
            start(link(h, s, ct))
        send_leaf(h, s - 1)

    def side(h):
        return remote(side_out.at[h], side_in.at[h], f_send.at[h], f_recv.at[h], partner)

    def sums_end(h):
        leaf(h, 3).wait_recv()
        link(h, 4, other).wait_recv()
        side_out[h] = (chain_in[h, 3, other].astype(F32) + leaf_in[h, 3, other].astype(F32)).astype(BF)
        start(side(h))
        own_copy(h).wait_recv()
        link(h, 4, k).wait_recv()
        return (
            acc[h, idx[1, 2 * z + k]]
            + own_in[h].astype(F32)
            + chain_in[h, 3, k].astype(F32)
            + leaf_in[h, 3, k].astype(F32)
        )

    forward(0)
    hand_over(0)
    sums_begin(0)
    forward(1)
    hand_over(1)
    sums_begin(1)
    for s in range(2, 5):
        sums_step(0, s)
        sums_step(1, s)
    halves = [sums_end(0), sums_end(1)]
    for h in range(2):
        side(h).wait_recv()
        halves[h] = (halves[h] + side_in[h].astype(F32)).astype(BF)
    aggregated = jnp.concatenate(halves, axis=1)

    preact = jnp.dot(aggregated, weight[...], preferred_element_type=F32)
    logistic = jax.nn.sigmoid(preact)
    pre_grad = (cot[...].astype(F32) * logistic * (1.0 + preact * (1.0 - logistic))).astype(BF)

    def twin(h, ct):
        tile = grads[h].at[z, ct]
        return remote(tile, tile, t_send.at[h], t_recv.at[h], partner)

    def chain(h, s, ct, at):
        tile = grads[h].at[at, ct]
        return remote(tile, tile, a_send.at[h, s - 1, ct], a_recv.at[h, s - 1, ct], two)

    def twig(h, s, at):
        tiles = grads[h].at[at]
        return remote(tiles, tiles, al_send.at[h, s - 1], al_recv.at[h, s - 1], one)

    def share(h, s, at):
        tiles = grads[h].at[at]
        return remote(tiles, tiles, q_send.at[h, s - 1], q_recv.at[h, s - 1], partner)

    def share_far(h, ct):
        tile = grads[h].at[chips[8], ct]
        return remote(tile, tile, q_send.at[h, 3], q_recv.at[h, 3], partner)

    def share_twig(h, s, at):
        tiles = grads[h].at[at]
        return remote(tiles, tiles, ql_send.at[h, s - 1], ql_recv.at[h, s - 1], partner)

    for h in range(2):
        grads[h][z, k] = lax.dot_general(
            pre_grad, weight[h * H : (h + 1) * H, :], (((1,), (1,)), ((), ())), preferred_element_type=F32
        ).astype(BF)
        start(twin(h, k))
        start(chain(h, 1, k, z))
    for h in range(2):
        twin(h, other).wait_recv()
        start(chain(h, 1, other, z))
        start(twig(h, 1, z))
    out[...] = (preact * logistic).astype(BF)
    w_loc[...] = lax.dot_general(
        aggregated, pre_grad, (((0,), (0,)), ((), ())), preferred_element_type=F32
    )
    for q in range(2):
        for p in range(NR):
            at = q * 128 + (p // 2) * 16
            w_sum[q, p] = w_loc[at : at + 16, (p % 2) * H : (p % 2 + 1) * H].astype(BF)
    w_swap = remote(w_sum.at[other], w_pair, wp_send, wp_recv, partner)
    w_swap.start()

    def advance(h, s):
        at = chips[-2 * s]
        if s < 4:
            for ct in (k, other):
                chain(h, s, ct, at).wait_recv()
                if s < 3 or ct is k:
                    start(chain(h, s + 1, ct, at))
            start(twig(h, s + 1, at))
            start(share(h, s, at))
        else:
            chain(h, 4, k, at).wait_recv()
            start(share_far(h, k))
        twig(h, s, chips[1 - 2 * s]).wait_recv()
        start(share_twig(h, s, chips[1 - 2 * s]))

    def shared(h):
        for s in range(1, 4):
            share(h, s, chips[2 * s]).wait_recv()
            share_twig(h, s, chips[2 * s - 1]).wait_recv()
        share_far(h, other).wait_recv()
        share_twig(h, 4, chips[7]).wait_recv()

    def w_spread(d):
        return remote(
            w_sum.at[k, lax.rem(r + d, NR)], w_x.at[d], wx_send.at[d], wx_recv.at[d], at_row(d)
        )

    def w_along(d):
        return remote(w_z.at[z], w_z.at[z], wz_send.at[d], wz_recv.at[d], at_z(d))

    def w_along_in(d):
        there = w_z.at[lax.rem(z - d + NZ, NZ)]
        return remote(there, there, wz_send.at[d], wz_recv.at[d], at_z(d))

    def w_share(d):
        return remote(w_all.at[r], w_all.at[r], wa_send.at[d], wa_recv.at[d], at_row(d))

    def w_share_in(d):
        there = w_all.at[lax.rem(r - d + NR, NR)]
        return remote(there, there, wa_send.at[d], wa_recv.at[d], at_row(d))

    def backward(h):
        def step(i, carry):
            for j in range(8):
                s = 8 * i + j
                row = idx[4, s]
                acc[h, s] = acc[h, idx[2, s]] + lax.dot_general(
                    vals[s],
                    grads[h][lax.div(row, 2), lax.rem(row, 2)],
                    (((0,), (0,)), ((), ())),
                    preferred_element_type=F32,
                )
            return carry

        lax.fori_loop(0, SLOTS // 8, step, 0)

        def give_back(d, carry):
            back_out[h, d] = acc[h, idx[3, lax.rem(r + d, NR)]].astype(BF)
            back(h)(d).start()
            return carry

        lax.fori_loop(1, NR, give_back, 0)

    def back(h):
        return lambda d: remote(
            back_out.at[h, d], back_in.at[h, d], b_send.at[h, d], b_recv.at[h, d], at_row(d)
        )

    def back_end(h):
        each(back(h), landed)
        total = lax.fori_loop(
            1, NR, lambda d, total: total + back_in[h, d].astype(F32), acc[h, idx[3, r]]
        )
        fgrad[:, h * H : (h + 1) * H] = total.astype(BF)

    advance(0, 1)
    w_swap.wait()
    w_sum[k] = (w_sum[k].astype(F32) + w_pair[...].astype(F32)).astype(BF)
    advance(1, 1)
    each(w_spread, begin)
    advance(0, 2)
    advance(1, 2)
    each(w_spread, landed)
    part = lax.fori_loop(
        1, NR, lambda d, total: total + w_x[d].astype(F32), w_sum[k, r].astype(F32)
    )
    w_z[z] = part.astype(BF)
    each(w_along, begin)
    advance(0, 3)
    advance(1, 3)
    advance(0, 4)
    shared(0)
    backward(0)
    advance(1, 4)
    each(w_along_in, landed)
    whole = lax.fori_loop(
        1, NZ, lambda i, total: total + w_z[i].astype(F32), w_z[0].astype(F32)
    )
    w_all[r] = whole * (1.0 / math.sqrt(NR * 2 * NZ * T))
    each(w_share, begin)
    shared(1)
    backward(1)

    each(w_share_in, landed)
    w_far = remote(w_all, w_other, wo_send, wo_recv, partner)
    w_far.start()
    for p in range(NR):
        at = pl.multiple_of(k * 128 + (p // 2) * 16, 16)
        wgrad[pl.ds(at, 16), (p % 2) * H : (p % 2 + 1) * H] = w_all[p]
    back_end(0)
    w_far.wait()
    for p in range(NR):
        at = pl.multiple_of(other * 128 + (p // 2) * 16, 16)
        wgrad[pl.ds(at, 16), (p % 2) * H : (p % 2 + 1) * H] = w_other[p]

    for copy in sent:
        copy.wait_send()
    for make in (gather(0), gather(1), w_spread, w_along, w_share):
        each(make, gone)
    back_end(1)
    for h in range(2):
        each(back(h), gone)


def in_hbm(array):
    return pltpu.with_memory_space_constraint(array, pltpu.HBM)


def on_device(features, weight, tile_values, tile_rows, tile_cols, tile_count, cotangent):
    width = features.shape[1]
    dma = pltpu.SemaphoreType.DMA
    vmem = pltpu.VMEM
    hbm = pl.BlockSpec(memory_space=pltpu.HBM)
    return pl.pallas_call(
        kernel,
        out_shape=(
            jax.ShapeDtypeStruct((T, width), BF),
            jax.ShapeDtypeStruct((T, width), BF),
            jax.ShapeDtypeStruct((width, width), F32),
        ),
        in_specs=[hbm] * 5 + [pl.BlockSpec(memory_space=pltpu.SMEM), hbm],
        out_specs=(pl.BlockSpec(memory_space=pltpu.VMEM),) * 3,
        scratch_shapes=[
            vmem((width, width), BF),
            vmem((SLOTS, T, T), BF),
            vmem((1, SLOTS), jnp.int32),
            vmem((1, SLOTS), jnp.int32),
            vmem((T, width), BF),
            vmem((8, 128), jnp.int32),
            pltpu.SMEM((8, 128), jnp.int32),
            vmem((COL_T, T, H), BF),
            vmem((COL_T, T, H), BF),
            vmem((2, SLOTS + 1, T, H), F32),
            vmem((2, 4, 2, 2, T, H), BF),
            vmem((2, 4, 2, 2, T, H), BF),
            vmem((2, T, H), BF),
            vmem((2, T, H), BF),
            vmem((2, T, H), BF),
            vmem((2, 4, 2, T, H), BF),
            vmem((2, 4, 2, T, H), BF),
            vmem((2, 4, 2, T, H), BF),
            vmem((2, T, H), BF),
            vmem((2, T, H), BF),
            vmem((NZ, 2, T, H), BF),
            vmem((NZ, 2, T, H), BF),
            vmem((2, NR, T, H), BF),
            vmem((2, NR, T, H), BF),
            vmem((width, width), F32),
            vmem((NR, 16, 128), BF),
            vmem((2, NR, 16, 128), BF),
            vmem((NR, 16, 128), BF),
            vmem((NZ, 16, 128), BF),
            vmem((NR, 16, 128), F32),
            vmem((NR, 16, 128), F32),
            dma((7,)),
            dma,
            dma((2, NR)), dma((2, NR)),
            dma((2, 4)), dma((2, 4)),
            dma((2,)), dma((2,)),
            dma((2, 4, 2)), dma((2, 4, 2)),
            dma((2, 4)), dma((2, 4)),
            dma((2,)), dma((2,)),
            dma((2, 4, 2)), dma((2, 4, 2)),
            dma((2, 4)), dma((2, 4)),
            dma((2, 4)), dma((2, 4)),
            dma((2, 4)), dma((2, 4)),
            dma((2,)), dma((2,)),
            dma((2, NR)), dma((2, NR)),
            dma, dma,
            dma((NR,)), dma((NR,)),
            dma((NZ,)), dma((NZ,)),
            dma((NR,)), dma((NR,)),
            dma, dma,
        ],
        compiler_params=pltpu.CompilerParams(
            collective_id=0, has_side_effects=True, vmem_limit_bytes=48 * 2**20
        ),
    )(
        in_hbm(features),
        in_hbm(weight),
        in_hbm(tile_values.reshape(SLOTS, T, T)),
        in_hbm(tile_rows.reshape(1, SLOTS)),
        in_hbm(tile_cols.reshape(1, SLOTS)),
        tile_count,
        in_hbm(cotangent),
    )


def solution(mesh):
    return jax.shard_map(
        on_device,
        mesh=mesh,
        in_specs=(
            P(("col", "row"), None),
            P(),
            P("row", "col", None, None, None),
            P("row", "col", None),
            P("row", "col", None),
            P("row", "col"),
            P(("row", "col"), None),
        ),
        out_specs=(P(("row", "col"), None), P(("col", "row"), None), P()),
        check_vma=False,
    )
```

time: 836 us -> 97.5 us (0.12)
  waiting for transfers between devices: 768 us -> 0 us
  Pallas kernels: 0 us -> 93.5 us
  other arithmetic: 29.1 us -> 0 us
  between operations: 13.8 us -> 1.29 us
  local copies, waits for them, and re-layouts: 13.4 us -> 1.96 us
  matrix products: 9.69 us -> 0 us
    psum x1 -> x0, waiting for transfers between devices: 437 us -> none  [on_device(): weight_grad = lax.psum(local_grad, ('row', 'col')) * scaling]
    reduce_scatter x2 -> x0, waiting for transfers between devices: 195 us -> none  [the longest x1 108 us: on_device(): lax.psum_scatter(partial_value.astype(jnp.bfloat16), 'col', scatter_dimen...]
    all_gather x2 -> x0, waiting for transfers between devices: 136 us -> none  [the longest x1 70.9 us: on_device(): grad_block = lax.all_gather(aggregate_grad, 'col', axis=0, tiled=True)]
    pallas_call x0 -> x1, Pallas kernels: none -> 93.5 us  [on_device(): pl.pallas_call(kernel, out_shape=(jax.ShapeDtypeStruct((T, width), BF), j...]
    scatter-add x4 -> x0, other arithmetic: 17.7 us -> none  [block_terms(): return total.at[target].add(products * active[:, None, None])]
    dot_general x7 -> x0, matrix products: 9.69 us -> none  [the longest x4 6.2 us: block_terms(): jnp.einsum(form, values, picked, preferred_element_type=jnp.float32)]
  transfers between devices with their start and end apart: 5 -> 0, of which waited for: 5 -> 0; matrix products, arithmetic and copies ran while one was open for 3% -> 0% of each run, Pallas kernels for 0% -> 0%
where the time goes in v2:
time: 97.5 us; the launch traced here: 96.8 us
  Pallas kernels  93.5 us (96%)
  local copies, waits for them, and re-layouts  1.96 us (2%)
  between operations  1.29 us (1%)
    pallas_call x1, Pallas kernels, on_device(): pl.pallas_call(kernel, out_shape=(jax.ShapeDtypeStruct((T, width), BF), j...  93.5 us
    unnamed x3, local copies, waits for them, and re-layouts  1.96 us

profile of v2, /device:TPU:1, one launch (start us, length us, event | category | flops | bytes accessed | tf_op | source)
XLA Modules:
  0.0 96.8 jit_solution(15456060098839168962)
XLA Ops:
  1.3 93.5 %shard_map.94 = (bf16[128,256]{1,0:T(8,128)(2,1)S(1)}, bf16[128,256]{1,0:T(8,128)(2,1)S(1)}, f32[256,256]{1,0:T(8,128)S(1)}) custom-call(bf16[128,256]{1,0:T(8,128)(2,1)} %feat.1, bf16[256,256]{1,0:T(8,128)(2,1)} %weight_hbm.1, bf16[32,128,128]{2,1,0:T(8,128)(2,1)} %bitcast.3, s32[1,32]{1,0:T(1,128)} %bitcast.4, s32[1,32]{1,0:T(1,128)} %bitcast.5, ...), custom_call_target="tpu_custom_call" | custom-call | tf_op jit(solution)/shard_map/pallas_call | solution.py:409
  94.8 0.6 copy.14
  95.5 0.6 copy.15
  96.1 0.7 copy.16

commit v3 on v2

--- a/solution.py
+++ b/solution.py
@@ -36,16 +36,18 @@
         down = jnp.sum(jnp.where(sub == lane, along, 0), axis=1, keepdims=True)
         table[base : base + 1, :SLOTS] = latest((down == along) & (sub < lane) & used)
         table[base + 1 : base + 2, :SLOTS] = latest((down == lane) & used)
-        table[4 + base // 2 : 5 + base // 2, :SLOTS] = ref[...]
+    table[4:5, :SLOTS] = rows[...]
+    table[5:6, :SLOTS] = lax.rem(cols[...], NY) * NX + lax.div(cols[...], NY)
+    table[6:7, :SLOTS] = cols[...]
 
 
 def kernel(
     feat, weight_hbm, vals_hbm, rows_hbm, cols_hbm, count, cot_hbm, out, fgrad, wgrad,
     weight, vals, rows, cols, cot, table, idx, panel_a, panel_b, acc, pair_out, pair_in, own_out, own_in, first, leaf_out,
-    chain_in, leaf_in, side_out, side_in, grads_a, grads_b, back_out, back_in,
+    chain_in, leaf_in, side_out, side_in, grads_a, grads_b, back_out, back_in, mid_out, mid_in,
     w_loc, w_pair, w_sum, w_x, w_z, w_all, w_other,
-    in_sem, idx_sem, g_send, g_recv, p_send, p_recv, o_send, o_recv, c_send, c_recv, l_send, l_recv, f_send, f_recv,
-    a_send, a_recv, al_send, al_recv, q_send, q_recv, ql_send, ql_recv, t_send, t_recv, b_send, b_recv,
+    in_sem, idx_sem, g_send, g_recv, gb_send, gb_recv, p_send, p_recv, o_send, o_recv, c_send, c_recv, l_send, l_recv, f_send, f_recv,
+    a_send, a_recv, al_send, al_recv, q_send, q_recv, ql_send, ql_recv, t_send, t_recv, b_send, b_recv, bm_send, bm_recv,
     wp_send, wp_recv, wx_send, wx_recv, wz_send, wz_recv, wa_send, wa_recv, wo_send, wo_recv,
 ):
     panel, grads = (panel_a, panel_b), (grads_a, grads_b)
@@ -55,6 +57,18 @@
     sigma = 1 - 2 * k
     partner = (r, 2 * z + other)
 
+    x, y = lax.div(r, NY), lax.rem(r, NY)
+    line = ((x, y), (y, x))
+
+    def row_of(h, a, b):
+        return a * NY + b if h == 0 else b * NY + a
+
+    def along_a(h, e):
+        return (row_of(h, lax.rem(line[h][0] + e, NX), line[h][1]), c)
+
+    def along_b(h, e):
+        return (row_of(h, line[h][0], lax.rem(line[h][1] + e, NX)), c)
+
     def at_row(d):
         return (lax.rem(r + d, NR), c)
 
@@ -84,7 +98,7 @@
     loads = [
         pltpu.make_async_copy(rows_hbm, rows, in_sem.at[0]),
         pltpu.make_async_copy(cols_hbm, cols, in_sem.at[1]),
-        pltpu.make_async_copy(feat.at[:, 0:H], panel[0].at[r], in_sem.at[2]),
+        pltpu.make_async_copy(feat.at[:, 0:H], panel[0].at[y * NX + x], in_sem.at[2]),
         pltpu.make_async_copy(feat.at[:, H : 2 * H], panel[1].at[r], in_sem.at[3]),
         pltpu.make_async_copy(vals_hbm, vals, in_sem.at[4]),
         pltpu.make_async_copy(weight_hbm, weight, in_sem.at[5]),
@@ -113,28 +127,32 @@
     to_idx.wait()
     pl.semaphore_wait(barrier, 2 * (NR - 1) + 1)
 
-    def gather(h):
-        mine = panel[h].at[r]
-        return lambda d: remote(mine, mine, g_send.at[h, d], g_recv.at[h, d], at_row(d))
-
-    def gathered(h):
-        def make(d):
-            theirs = panel[h].at[lax.rem(r - d + NR, NR)]
-            return remote(theirs, theirs, g_send.at[h, d], g_recv.at[h, d], at_row(d))
-
-        return make
+    def gather_a(h, e, a):
+        tile = panel[h].at[line[h][1] * NX + a]
+        return remote(tile, tile, g_send.at[h, e - 1], g_recv.at[h, e - 1], along_a(h, e))
+
+    def gather_b(h, e, b):
+        tiles = panel[h].at[pl.ds(b * NX, NX)]
+        return remote(tiles, tiles, gb_send.at[h, e - 1], gb_recv.at[h, e - 1], along_b(h, e))
 
     for h in range(2):
-        each(gather(h), begin)
+        for e in (2, 1, 3):
+            start(gather_a(h, e, line[h][0]))
+    for h in range(2):
+        for e in (1, 3, 2):
+            gather_a(h, e, lax.rem(line[h][0] - e + NX, NX)).wait_recv()
+        for e in (2, 1, 3):
+            start(gather_b(h, e, line[h][1]))
 
     def forward(h):
-        each(gathered(h), landed)
+        for e in (1, 3, 2):
+            gather_b(h, e, lax.rem(line[h][1] - e + NX, NX)).wait_recv()
 
         def step(i, carry):
             for j in range(8):
                 s = 8 * i + j
                 acc[h, s] = acc[h, idx[0, s]] + jnp.dot(
-                    vals[s], panel[h][idx[5, s]], preferred_element_type=F32
+                    vals[s], panel[h][idx[5 + h, s]], preferred_element_type=F32
                 )
             return carry
 
@@ -329,23 +347,40 @@
 
         lax.fori_loop(0, SLOTS // 8, step, 0)
 
-        def give_back(d, carry):
-            back_out[h, d] = acc[h, idx[3, lax.rem(r + d, NR)]].astype(BF)
-            back(h)(d).start()
-            return carry
-
-        lax.fori_loop(1, NR, give_back, 0)
-
-    def back(h):
-        return lambda d: remote(
-            back_out.at[h, d], back_in.at[h, d], b_send.at[h, d], b_recv.at[h, d], at_row(d)
+        for e in (2, 1, 3):
+            for a in range(NX):
+                last = idx[3, row_of(h, a, lax.rem(line[h][1] + e, NX))]
+                back_out[h, e - 1, a] = acc[h, last].astype(BF)
+            start(back(h, e))
+
+    def back(h, e):
+        return remote(
+            back_out.at[h, e - 1], back_in.at[h, e - 1], b_send.at[h, e - 1], b_recv.at[h, e - 1], along_b(h, e)
         )
 
+    def middle(h, e):
+        return remote(
+            mid_out.at[h, e - 1], mid_in.at[h, e - 1], bm_send.at[h, e - 1], bm_recv.at[h, e - 1], along_a(h, e)
+        )
+
+    def line_sum(h, a):
+        total = acc[h, idx[3, row_of(h, a, line[h][1])]]
+        for e in range(3):
+            total = total + back_in[h, e, a].astype(F32)
+        return total
+
+    def back_middle(h):
+        for e in (1, 3, 2):
+            back(h, e).wait_recv()
+        for e in (2, 1, 3):
+            mid_out[h, e - 1] = line_sum(h, lax.rem(line[h][0] + e, NX)).astype(BF)
+            start(middle(h, e))
+
     def back_end(h):
-        each(back(h), landed)
-        total = lax.fori_loop(
-            1, NR, lambda d, total: total + back_in[h, d].astype(F32), acc[h, idx[3, r]]
-        )
+        total = line_sum(h, line[h][0])
+        for e in (1, 3, 2):
+            middle(h, e).wait_recv()
+            total = total + mid_in[h, e - 1].astype(F32)
         fgrad[:, h * H : (h + 1) * H] = total.astype(BF)
 
     advance(0, 1)
@@ -375,26 +410,25 @@
     each(w_share, begin)
     shared(1)
     backward(1)
+    back_middle(0)
 
     each(w_share_in, landed)
     w_far = remote(w_all, w_other, wo_send, wo_recv, partner)
-    w_far.start()
+    start(w_far)
     for p in range(NR):
         at = pl.multiple_of(k * 128 + (p // 2) * 16, 16)
         wgrad[pl.ds(at, 16), (p % 2) * H : (p % 2 + 1) * H] = w_all[p]
+    back_middle(1)
     back_end(0)
-    w_far.wait()
+    w_far.wait_recv()
     for p in range(NR):
         at = pl.multiple_of(other * 128 + (p // 2) * 16, 16)
         wgrad[pl.ds(at, 16), (p % 2) * H : (p % 2 + 1) * H] = w_other[p]
-
+    for make in (w_spread, w_along, w_share):
+        each(make, gone)
+    back_end(1)
     for copy in sent:
         copy.wait_send()
-    for make in (gather(0), gather(1), w_spread, w_along, w_share):
-        each(make, gone)
-    back_end(1)
-    for h in range(2):
-        each(back(h), gone)
 
 
 def in_hbm(array):
@@ -438,8 +472,10 @@
             vmem((2, T, H), BF),
             vmem((NZ, 2, T, H), BF),
             vmem((NZ, 2, T, H), BF),
-            vmem((2, NR, T, H), BF),
-            vmem((2, NR, T, H), BF),
+            vmem((2, 3, NX, T, H), BF),
+            vmem((2, 3, NX, T, H), BF),
+            vmem((2, 3, T, H), BF),
+            vmem((2, 3, T, H), BF),
             vmem((width, width), F32),
             vmem((NR, 16, 128), BF),
             vmem((2, NR, 16, 128), BF),
@@ -449,7 +485,8 @@
             vmem((NR, 16, 128), F32),
             dma((7,)),
             dma,
-            dma((2, NR)), dma((2, NR)),
+            dma((2, 3)), dma((2, 3)),
+            dma((2, 3)), dma((2, 3)),
             dma((2, 4)), dma((2, 4)),
             dma((2,)), dma((2,)),
             dma((2, 4, 2)), dma((2, 4, 2)),
@@ -460,7 +497,8 @@
             dma((2, 4)), dma((2, 4)),
             dma((2, 4)), dma((2, 4)),
             dma((2,)), dma((2,)),
-            dma((2, NR)), dma((2, NR)),
+            dma((2, 3)), dma((2, 3)),
+            dma((2, 3)), dma((2, 3)),
             dma, dma,
             dma((NR,)), dma((NR,)),
             dma((NZ,)), dma((NZ,)),

time: 97.5 us -> 92.5 us (0.949)
  Pallas kernels: 93.5 us -> 89.1 us
    pallas_call x1, Pallas kernels: 93.5 us -> 89.1 us  [on_device(): pl.pallas_call(kernel, out_shape=(jax.ShapeDtypeStruct((T, width), BF), j...]
where the time goes in v3:
time: 92.5 us; the launch traced here: 92.3 us
  Pallas kernels  89.1 us (96%)
  local copies, waits for them, and re-layouts  1.96 us (2%)
  between operations  1.29 us (1%)
    pallas_call x1, Pallas kernels, on_device(): pl.pallas_call(kernel, out_shape=(jax.ShapeDtypeStruct((T, width), BF), j...  89.1 us
    unnamed x3, local copies, waits for them, and re-layouts  1.96 us

profile of v3, /device:TPU:1, one launch (start us, length us, event | category | flops | bytes accessed | tf_op | source)
XLA Modules:
  0.0 92.3 jit_solution(15433983304411528207)
XLA Ops:
  1.3 89.1 %shard_map.94 = (bf16[128,256]{1,0:T(8,128)(2,1)S(1)}, bf16[128,256]{1,0:T(8,128)(2,1)S(1)}, f32[256,256]{1,0:T(8,128)S(1)}) custom-call(bf16[128,256]{1,0:T(8,128)(2,1)} %feat.1, bf16[256,256]{1,0:T(8,128)(2,1)} %weight_hbm.1, bf16[32,128,128]{2,1,0:T(8,128)(2,1)} %bitcast.3, s32[1,32]{1,0:T(1,128)} %bitcast.4, s32[1,32]{1,0:T(1,128)} %bitcast.5, ...), custom_call_target="tpu_custom_call" | custom-call | tf_op jit(solution)/shard_map/pallas_call | solution.py:443
  90.3 0.6 copy.14
  91.0 0.6 copy.15
  91.6 0.7 copy.16

commit v4 on v3

--- a/solution.py
+++ b/solution.py
@@ -108,13 +108,13 @@
         load.start()
     barrier = pltpu.get_barrier_semaphore()
 
-    def greet(d, carry):
-        pl.semaphore_signal(barrier, inc=1, device_id=at_z(d), device_id_type=MESH)
-        pl.semaphore_signal(barrier, inc=1, device_id=at_row(d), device_id_type=MESH)
-        return carry
-
-    lax.fori_loop(1, NR, greet, 0)
-    pl.semaphore_signal(barrier, inc=1, device_id=partner, device_id_type=MESH)
+    greeted = [partner]
+    for e in (2, 1, 3):
+        greeted += [along_a(0, e), along_b(0, e)]
+    for e in (2, NZ - 2, 1, NZ - 1):
+        greeted.append(at_z(e))
+    for device in greeted:
+        pl.semaphore_signal(barrier, inc=1, device_id=device, device_id_type=MESH)
     for h in range(2):
         acc[h, SLOTS] = jnp.zeros((T, H), F32)
     loads[0].wait()
@@ -122,10 +122,9 @@
     slot_tables(rows, cols, count[0, 0], table)
     to_idx = pltpu.make_async_copy(table, idx, idx_sem)
     to_idx.start()
-    for load in loads[2:]:
+    for load in loads[2:4]:
         load.wait()
-    to_idx.wait()
-    pl.semaphore_wait(barrier, 2 * (NR - 1) + 1)
+    pl.semaphore_wait(barrier, len(greeted))
 
     def gather_a(h, e, a):
         tile = panel[h].at[line[h][1] * NX + a]
@@ -227,6 +226,9 @@
             + leaf_in[h, 3, k].astype(F32)
         )
 
+    for load in loads[4:]:
+        load.wait()
+    to_idx.wait()
     forward(0)
     hand_over(0)
     sums_begin(0)

time: 92.5 us -> 91.1 us (0.985)
  Pallas kernels: 89.1 us -> 87.7 us
    pallas_call x1, Pallas kernels: 89.1 us -> 87.7 us  [on_device(): pl.pallas_call(kernel, out_shape=(jax.ShapeDtypeStruct((T, width), BF), j...]
where the time goes in v4:
time: 91.1 us; the launch traced here: 91 us
  Pallas kernels  87.7 us (96%)
  local copies, waits for them, and re-layouts  1.96 us (2%)
  between operations  1.29 us (1%)
    pallas_call x1, Pallas kernels, on_device(): pl.pallas_call(kernel, out_shape=(jax.ShapeDtypeStruct((T, width), BF), j...  87.7 us
    unnamed x3, local copies, waits for them, and re-layouts  1.96 us

profile of v4, /device:TPU:1, one launch (start us, length us, event | category | flops | bytes accessed | tf_op | source)
XLA Modules:
  0.0 91.0 jit_solution(2925563153198202413)
XLA Ops:
  1.3 87.7 %shard_map.94 = (bf16[128,256]{1,0:T(8,128)(2,1)S(1)}, bf16[128,256]{1,0:T(8,128)(2,1)S(1)}, f32[256,256]{1,0:T(8,128)S(1)}) custom-call(bf16[128,256]{1,0:T(8,128)(2,1)} %feat.1, bf16[256,256]{1,0:T(8,128)(2,1)} %weight_hbm.1, bf16[32,128,128]{2,1,0:T(8,128)(2,1)} %bitcast.3, s32[1,32]{1,0:T(1,128)} %bitcast.4, s32[1,32]{1,0:T(1,128)} %bitcast.5, ...), custom_call_target="tpu_custom_call" | custom-call | tf_op jit(solution)/shard_map/pallas_call | solution.py:445
  89.0 0.6 copy.14
  89.6 0.6 copy.15
  90.3 0.7 copy.16

commit v5 on v4

--- a/solution.py
+++ b/solution.py
@@ -198,7 +198,6 @@
         send_leaf(h, 0)
 
     def sums_step(h, s):
-        pair(h, s - 1).wait_recv()
         leaf(h, s - 2).wait_recv()
         for ct in (other, k):
             total = both(h, 10 - 2 * s, ct) + leaf_in[h, s - 2, ct].astype(F32)
@@ -207,7 +206,6 @@
                 total = total + chain_in[h, s - 2, ct].astype(F32)
             chain_in[h, s - 2, ct] = total.astype(BF)
             start(link(h, s, ct))
-        send_leaf(h, s - 1)
 
     def side(h):
         return remote(side_out.at[h], side_in.at[h], f_send.at[h], f_recv.at[h], partner)
@@ -236,6 +234,9 @@
     hand_over(1)
     sums_begin(1)
     for s in range(2, 5):
+        for h in range(2):
+            pair(h, s - 1).wait_recv()
+            send_leaf(h, s - 1)
         sums_step(0, s)
         sums_step(1, s)
     halves = [sums_end(0), sums_end(1)]

time: 91.1 us -> 88.4 us (0.970)
  Pallas kernels: 87.7 us -> 85 us
    pallas_call x1, Pallas kernels: 87.7 us -> 85 us  [on_device(): pl.pallas_call(kernel, out_shape=(jax.ShapeDtypeStruct((T, width), BF), j...]
where the time goes in v5:
time: 88.4 us; the launch traced here: 88.2 us
  Pallas kernels  85 us (96%)
  local copies, waits for them, and re-layouts  1.96 us (2%)
  between operations  1.29 us (1%)
    pallas_call x1, Pallas kernels, on_device(): pl.pallas_call(kernel, out_shape=(jax.ShapeDtypeStruct((T, width), BF), j...  85 us
    unnamed x3, local copies, waits for them, and re-layouts  1.96 us

profile of v5, /device:TPU:1, one launch (start us, length us, event | category | flops | bytes accessed | tf_op | source)
XLA Modules:
  0.0 88.2 jit_solution(7917956335801638208)
XLA Ops:
  1.3 85.0 %shard_map.94 = (bf16[128,256]{1,0:T(8,128)(2,1)S(1)}, bf16[128,256]{1,0:T(8,128)(2,1)S(1)}, f32[256,256]{1,0:T(8,128)S(1)}) custom-call(bf16[128,256]{1,0:T(8,128)(2,1)} %feat.1, bf16[256,256]{1,0:T(8,128)(2,1)} %weight_hbm.1, bf16[32,128,128]{2,1,0:T(8,128)(2,1)} %bitcast.3, s32[1,32]{1,0:T(1,128)} %bitcast.4, s32[1,32]{1,0:T(1,128)} %bitcast.5, ...), custom_call_target="tpu_custom_call" | custom-call | tf_op jit(solution)/shard_map/pallas_call | solution.py:446
  86.3 0.6 copy.14
  86.9 0.6 copy.15
  87.5 0.7 copy.16
